TPU v7x, 256 devices: a whole 4x4x8 slice. The times are simulated.
256 devices in a mesh: rep: 16 (over y, x_lo, core), exp: 16 (over z, x_hi).
Axes of the slice: x: 4 (x_hi: 2, x_lo: 2; x = x_hi * 2 + x_lo), y: 4, z: 8, core: 2. Of those that a mesh axis runs over, the one named last changes fastest.
Arguments:
- acts: bfloat16 [16, 16, 64, 2, 2048], P('rep', 'exp'), may hold values from -6 to 6
- cotangent: bfloat16 [16, 64, 2, 32, 768], P('rep', 'exp'), may hold values from -0.25 to 0.25
- counts: int32 [16, 16, 64], P('rep', 'exp'), may hold values from 1 to 2, as said below
- momentum: bfloat16 [2048, 64, 2, 768], P('rep', 'exp'), may hold values from -24 to 24
Outputs:
- new_momentum: bfloat16 [2048, 64, 2, 768], P('rep', 'exp')
- update: bfloat16 [2048, 64, 2, 768], P('rep', 'exp')
Inputs may be any that keep to these rules, and one draw needn't show every extreme that they name: `counts`: in every draw some source device sends exactly 2 tokens to some expert.
All inputs are finite; a program needn't handle non-finite values.
Results may differ from a plain program's by a relative error of at most 0.02.
Values may be sent and summed in bfloat16 or wider, within the bound.
A program may use at most 128 MiB of HBM per device.

v0:
```python
import math

import jax
import jax.numpy as jnp
from jax import lax
from jax.sharding import PartitionSpec as P

ITERS = 2


coef_a = 3.4445
coef_b = -4.775
coef_c = 2.0315
decay_rate = 0.95
norm_eps = 1e-07


def swapped(value, axis, distance):
    mask = 2**distance
    pairs = [(source, source ^ mask) for source in range(lax.axis_size(axis))]
    return lax.ppermute(value, axis, pairs)


def on_device(acts, cotangent, counts, momentum):
    slot_count = acts.shape[3]
    slot_index = lax.broadcasted_iota(jnp.int32, (1, 1, 1, slot_count, 1), 3)
    live_rows = slot_index < counts[:, :, :, None, None]
    live = jnp.where(live_rows, acts, jnp.zeros_like(acts))
    routed = lax.all_to_all(live, "exp", split_axis=2, concat_axis=1, tiled=True)
    groups_here = routed.shape[1]
    experts_here = momentum.shape[1]
    shard_rows = momentum.shape[0]
    hidden = momentum.shape[3]
    grads_out = cotangent[0].reshape(experts_here, 2, groups_here, slot_count, hidden)
    feature_cols = routed[0]
    grad = lax.psum_scatter(
        jnp.einsum(
            "secd,ekscf->dekf", feature_cols, grads_out, preferred_element_type=jnp.float32
        ).astype(jnp.bfloat16),
        "rep",
        scatter_dimension=0,
        tiled=True,
    ).astype(jnp.float32)
    mom_new = decay_rate * momentum.astype(jnp.float32) + grad
    new_momentum = mom_new.astype(jnp.bfloat16)
    nest = (grad + decay_rate * mom_new).astype(jnp.bfloat16)
    matrices = nest.transpose(1, 2, 0, 3).reshape(2 * experts_here, shard_rows, hidden)
    replicas = lax.axis_size("rep")
    stride = replicas // (2 * experts_here)
    pieces = shard_rows // stride
    send_rows = matrices.reshape(replicas, pieces, hidden)
    owned = lax.all_to_all(send_rows, "rep", split_axis=0, concat_axis=0, tiled=True).reshape(
        replicas * pieces, hidden
    )
    values = owned.astype(jnp.float32)
    total_sq = jnp.sum(values * values)
    total_sq = total_sq + swapped(total_sq, "rep", 0)
    ortho = (values / (jnp.sqrt(total_sq) + norm_eps)).astype(jnp.bfloat16)
    ortho = lax.optimization_barrier(ortho)
    for sweep in range(ITERS):
        gram_part = jnp.dot(ortho.T, ortho, preferred_element_type=jnp.float32)
        gram_part = gram_part + swapped(gram_part.astype(jnp.bfloat16), "rep", 0).astype(
            gram_part.dtype
        )
        gram_mat = lax.optimization_barrier(gram_part.astype(jnp.bfloat16))
        square = jnp.dot(gram_mat, gram_mat, preferred_element_type=jnp.float32)
        poly_mat = (coef_b * gram_mat.astype(jnp.float32) + coef_c * square).astype(jnp.bfloat16)
        ortho = (
            coef_a * ortho.astype(jnp.float32)
            + jnp.dot(ortho, poly_mat, preferred_element_type=jnp.float32)
        ).astype(jnp.bfloat16)
        ortho = lax.optimization_barrier(ortho)
    returned = lax.all_to_all(
        ortho.reshape(replicas, pieces, hidden), "rep", split_axis=0, concat_axis=0, tiled=True
    )
    mine = returned.reshape(2 * experts_here, shard_rows, hidden)
    scaled = (math.sqrt(replicas * shard_rows) * mine.astype(jnp.float32)).astype(jnp.bfloat16)
    update = scaled.reshape(experts_here, 2, shard_rows, hidden).transpose(2, 0, 1, 3)
    return (new_momentum, update)


def solution(mesh):
    in_specs = (
        P("rep", "exp", None, None, None),
        P("rep", "exp", None, None, None),
        P("rep", "exp", None),
        P("rep", "exp", None, None),
    )
    out_specs = (P("rep", "exp", None, None), P("rep", "exp", None, None))
    return jax.shard_map(
        on_device, mesh=mesh, in_specs=in_specs, out_specs=out_specs, check_vma=False
    )
```

profile of v0, /device:TPU:1, one launch (start us, length us, event | category | flops | bytes accessed | tf_op | source)
XLA Modules:
  0.0 408.7 jit_solution(11821939603324461272)
XLA Ops:
  7.2 0.0 copy-start.3
  7.2 0.8 iota_compare_fusion
  8.0 2.4 broadcast_select_fusion
  10.3 11.6 %all-to-all-start = ((bf16[1,1,64,2,2048]{4,3,1,0,2:T(2,128)(2,1)}), bf16[1,1,64,2,2048]{4,3,1,0,2:T(2,128)(2,1)S(1)}, u32[]{:S(2)}, u32[]{:S(2)}) async-start(bf16[1,1,64,2,2048]{4,3,1,0,2:T(2,128)(2,1)} %broadcast_select_fusion), calls=%async_computation | async-start | bytes 1048576 | tf_op jit(solution)/shard_map/all_to_all | solution.py:29
  21.9 0.0 reduce-scatter.2.cloned.1.call-start
  22.0 0.0 copy-done.3
  22.0 0.1 reshape_squeeze.3
  22.1 16.9 %all-to-all-done = bf16[1,1,64,2,2048]{4,3,1,0,2:T(2,128)(2,1)S(1)} async-done(((bf16[1,1,64,2,2048]{4,3,1,0,2:T(2,128)(2,1)}), bf16[1,1,64,2,2048]{4,3,1,0,2:T(2,128)(2,1)S(1)}, u32[]{:S(2)}, u32[]{:S(2)}) %all-to-all-start) | async-done | bytes 524320 | tf_op jit(solution)/shard_map/all_to_all | solution.py:29
  39.0 11.7 %fusion = bf16[2048,4,2,768]{3,0,2,1:T(8,128)(2,1)} fusion(bf16[16,4,2,2048,1]{3,2,1,0,4:T(2,128)(2,1)S(1)} %bitcast.35, bf16[4,2,16,2,768]{4,3,2,1,0:T(2,128)(2,1)S(1)} %reshape_squeeze.3), kind=kOutput, calls=%fused_computation.1 | convolution fusion | flops 817889280 | bytes 26083328 | tf_op jit(solution)/shard_map/secd,ekscf->dekf/dot_general | solution.py:37
  50.7 0.0 copy-start
  50.7 0.0 reduce-scatter.2.cloned.1.call-update
  50.8 264.8 %reduce-scatter.2.cloned.1.call-done = bf16[128,4,2,768]{3,0,2,1:T(8,128)(2,1)} async-done(((bf16[2048,4,2,768]{3,0,2,1:T(8,128)(2,1)}), bf16[128,4,2,768]{3,0,2,1:T(8,128)(2,1)}) %reduce-scatter.2.cloned.1.call-update) | async-done | bytes 1572880 | tf_op jit(solution)/shard_map/reduce_scatter | solution.py:36
  315.6 0.0 copy-done
  315.6 2.2 fusion.1
  317.8 25.9 %all_to_all.19 = bf16[16,64,768]{2,1,0:T(8,128)(2,1)S(1)} all-to-all(bf16[16,64,768]{2,1,0:T(8,128)(2,1)S(1)} %bitcast.34), channel_id=1, replica_groups=mesh['rep'=16,'exp'=16] {'rep'}, dimensions={0} | all-to-all | bytes 3145728 | tf_op jit(solution)/shard_map/all_to_all | solution.py:52
  343.7 1.4 fusion.2
  345.1 1.2 collective-permute-start
  346.3 1.0 collective-permute-done
  348.5 0.3 fusion.3
  348.9 0.0 copy-start.1
  348.9 1.5 fusion.11
  350.3 0.0 copy-done.1
  350.4 0.5 collective-permute-start.1
  350.9 2.6 collective-permute-done.1
  353.5 0.0 copy-start.2
  353.5 1.3 add_convert_fusion.5
  354.8 0.5 copy-done.2
  355.3 5.9 %add_convert_fusion.1 = bf16[1024,768]{1,0:T(8,128)(2,1)} fusion(bf16[1024,768]{1,0:T(8,128)(2,1)S(1)} %bitcast.38, bf16[768,768]{1,0:T(8,128)(2,1)} %add_convert_fusion.5), kind=kOutput, calls=%fused_computation.11 | convolution fusion | flops 2120024064 | bytes 4325376 | tf_op jit(solution)/shard_map/dot_general | solution.py:70
  361.2 3.5 fusion.12
  364.7 0.4 collective-permute-start.2
  365.0 2.6 collective-permute-done.2
  367.6 0.3 add_convert_fusion.3
  367.9 5.5 %add_convert_fusion = bf16[1024,768]{1,0:T(8,128)(2,1)} fusion(bf16[1024,768]{1,0:T(8,128)(2,1)} %add_convert_fusion.1, bf16[768,768]{1,0:T(8,128)(2,1)S(1)} %add_convert_fusion.3), kind=kOutput, calls=%fused_computation.10 | convolution fusion | flops 2120024064 | bytes 4325376 | tf_op jit(solution)/shard_map/dot_general | solution.py:70
  373.4 3.8 all-to-all-start.2
  377.2 2.8 copy.18
  379.9 18.8 %all-to-all-done.2 = bf16[16,64,768]{2,1,0:T(8,128)(2,1)S(1)} async-done(((bf16[16,64,768]{2,1,0:T(8,128)(2,1)}), bf16[16,64,768]{2,1,0:T(8,128)(2,1)S(1)}, u32[]{:S(2)}, u32[]{:S(2)}) %all-to-all-start.2) | async-done | bytes 1572896 | tf_op jit(solution)/shard_map/all_to_all | solution.py:73
  398.8 0.3 multiply_convert_fusion
  399.1 2.8 copy.19
Async XLA Ops:
  7.2 14.8 %copy-start.3 = (bf16[1,4,2,32,768]{4,3,2,1,0:T(8,128)(2,1)S(1)}, bf16[1,4,2,32,768]{4,3,2,1,0:T(8,128)(2,1)}, u32[]{:S(2)}) copy-start(bf16[1,4,2,32,768]{4,3,2,1,0:T(8,128)(2,1)} %param.5) | copy-start | bytes 1179652
  10.3 28.7 %all-to-all-start = ((bf16[1,1,64,2,2048]{4,3,1,0,2:T(2,128)(2,1)}), bf16[1,1,64,2,2048]{4,3,1,0,2:T(2,128)(2,1)S(1)}, u32[]{:S(2)}, u32[]{:S(2)}) async-start(bf16[1,1,64,2,2048]{4,3,1,0,2:T(2,128)(2,1)} %broadcast_select_fusion), calls=%async_computation | async-start | bytes 1048576 | tf_op jit(solution)/shard_map/all_to_all | solution.py:29
  21.9 293.6 %reduce-scatter.2.cloned.1.call-start = ((), (), s32[]{:S(2)}) async-start(), calls=%async_computation.4 | async-start | bytes 26738688 | tf_op jit(solution)/shard_map/reduce_scatter | solution.py:36
  50.7 264.8 %copy-start = (bf16[128,4,2,768]{3,2,1,0:T(2,128)(2,1)S(1)}, bf16[128,4,2,768]{3,2,1,0:T(2,128)(2,1)}, u32[]{:S(2)}) copy-start(bf16[128,4,2,768]{3,2,1,0:T(2,128)(2,1)} %param.7) | copy-start | bytes 4718596
  345.1 2.1 collective-permute-start
  348.9 1.5 copy-start.1
  350.4 3.1 collective-permute-start.1
  353.5 1.8 copy-start.2
  364.7 2.9 collective-permute-start.2
  373.4 25.4 %all-to-all-start.2 = ((bf16[16,64,768]{2,1,0:T(8,128)(2,1)}), bf16[16,64,768]{2,1,0:T(8,128)(2,1)S(1)}, u32[]{:S(2)}, u32[]{:S(2)}) async-start(bf16[16,64,768]{2,1,0:T(8,128)(2,1)} %bitcast.36), calls=%async_computation.3 | async-start | bytes 3145728 | tf_op jit(solution)/shard_map/all_to_all | solution.py:73
Sparse Core Ops, SparseCore 0:
  50.9 264.6 reduce-scatter.1
where the time goes:
time: 409 us
  waiting for transfers between devices  307 us (75%)
  matrix products  28 us (7%)
  blocking collectives  25.9 us (6%)
  starting transfers between devices  17.5 us (4%)
  between operations  15.4 us (4%)
  other arithmetic  9 us (2%)
  local copies, waits for them, and re-layouts  6.22 us (2%)
    reduce_scatter x1, waiting for transfers between devices, on_device(): lax.psum_scatter(jnp.einsum('secd,ekscf->dekf', feature_cols, grads_out,...  265 us
    all_to_all x1, blocking collectives, on_device(): lax.all_to_all(send_rows, 'rep', split_axis=0, concat_axis=0, tiled=True)  25.9 us
    all_to_all x1, waiting for transfers between devices, on_device(): lax.all_to_all(ortho.reshape(replicas, pieces, hidden), 'rep', split_axis...  18.8 us
    all_to_all x1, waiting for transfers between devices, on_device(): lax.all_to_all(live, 'exp', split_axis=2, concat_axis=1, tiled=True)  16.9 us
    dot_general x1, matrix products, on_device(): jnp.einsum('secd,ekscf->dekf', feature_cols, grads_out, preferred_element...  11.7 us
    all_to_all x1, starting transfers between devices, on_device(): lax.all_to_all(live, 'exp', split_axis=2, concat_axis=1, tiled=True)  11.6 us
    dot_general x2, matrix products, on_device(): jnp.dot(ortho, poly_mat, preferred_element_type=jnp.float32)  11.4 us
  transfers between devices with their start and end apart: 6, of which 6 were waited for; matrix products, arithmetic and copies ran while one was open for 1% of the time, Pallas kernels for 0%

commit v1 on v0

v1 whole, which is shorter than its diff:
```python
import functools
import math

import jax
import jax.numpy as jnp
from jax import lax
from jax.experimental import pallas as pl
from jax.experimental.pallas import tpu as pltpu
from jax.sharding import PartitionSpec as P

coef_a = 3.4445
coef_b = -4.775
coef_c = 2.0315
decay_rate = 0.95
norm_eps = 1e-07

REP = 16
EXP = 16
CHIPS = 8
YS = 4
EXPERTS_HERE = 4
SLOTS = 2
WIDTH = 2048
HALF = WIDTH // 2
SHARD = 128
HIDDEN = 768
TOKENS = 32
TILE = 256

MESH = pl.DeviceIdType.MESH
f32 = jnp.float32
bf16 = jnp.bfloat16


def remote(src, dst, send_sem, recv_sem, rep, exp):
    return pltpu.make_async_remote_copy(
        src_ref=src,
        dst_ref=dst,
        send_sem=send_sem,
        recv_sem=recv_sem,
        device_id=(rep, exp),
        device_id_type=MESH,
    )


def dot32(left, right):
    return jnp.dot(left, right, preferred_element_type=f32)


def dot_rows(left, right):
    return lax.dot_general(left, right, (((0,), (0,)), ((), ())), preferred_element_type=f32)


def kernel(
    tok_in,
    cot_in,
    mom_in,
    new_out,
    upd_out,
    tok_r,
    t2_s,
    t2_r,
    cot_r,
    mom_r,
    new_s,
    nest_s,
    upd_s,
    gram_s,
    gram_r,
    gram_f,
    sq_s,
    sq_r,
    g0,
    bend0,
    step,
    g1,
    bend1,
    both,
    tok_ss,
    tok_rs,
    cot_ss,
    cot_rs,
    mom_ss,
    mom_rs,
    t2_ss,
    t2_rs,
    new_ss,
    new_rs,
    upd_ss,
    upd_rs,
    pair_ss,
    pair_rs,
    local_sem,
):
    rep = lax.axis_index("rep")
    exp = lax.axis_index("exp")
    chip = rep // 2
    core = lax.rem(rep, 2)
    y = rep // 4
    x = lax.rem(chip, 2)
    peer = y * 2 + core
    rep_x = y * 4 + (1 - x) * 2 + core
    rep_core = chip * 2 + (1 - core)

    def signal(to_rep, to_exp):
        pl.semaphore_signal(
            pltpu.get_barrier_semaphore(), inc=1, device_id=(to_rep, to_exp), device_id_type=MESH
        )

    def greet(i, carry):
        signal(rep, lax.rem(exp + i, EXP))
        signal(lax.rem(rep + i, REP), exp)
        signal(rep_x, lax.rem(exp + i, EXP))
        return carry

    lax.fori_loop(1, 16, greet, 0)
    pl.semaphore_wait(pltpu.get_barrier_semaphore(), 45)

    def tok_copy(i, other):
        to = lax.rem(exp + i, EXP)
        return remote(
            tok_in.at[to],
            tok_r.at[x, exp],
            tok_ss.at[other, i],
            tok_rs.at[x, exp],
            rep_x if other else rep,
            to,
        )

    def cot_copy(i):
        to = lax.rem(rep + i, REP)
        return remote(
            cot_in.at[to // 2], cot_r.at[peer, x], cot_ss.at[i], cot_rs.at[rep], to, exp
        )

    def mom_copy(i):
        to = lax.rem(chip + i, CHIPS)
        return remote(
            mom_in.at[to], mom_r.at[chip], mom_ss.at[i], mom_rs.at[chip], to * 2 + core, exp
        )

    tok_local = pltpu.make_async_copy(tok_in.at[exp], tok_r.at[x, exp], local_sem.at[0])
    cot_local = pltpu.make_async_copy(cot_in.at[chip], cot_r.at[peer, x], local_sem.at[1])
    mom_local = pltpu.make_async_copy(mom_in.at[chip], mom_r.at[chip], local_sem.at[2])

    tok_copy(0, 1).start()

    def start_tok(i, carry):
        tok_copy(i, 0).start()
        tok_copy(i, 1).start()
        return carry

    lax.fori_loop(1, EXP, start_tok, 0)

    def start_cot(i, carry):
        cot_copy(i).start()
        return carry

    lax.fori_loop(1, REP, start_cot, 0)

    def start_mom(i, carry):
        mom_copy(i).start()
        return carry

    lax.fori_loop(1, CHIPS, start_mom, 0)
    tok_local.start()
    cot_local.start()
    mom_local.start()

    out_row = lax.broadcasted_iota(jnp.int32, (SHARD, SHARD), 0)
    in_row = lax.broadcasted_iota(jnp.int32, (SHARD, SHARD), 1)
    wanted = (
        lax.rem(out_row // SLOTS, EXP) * (EXPERTS_HERE * SLOTS)
        + (out_row // TOKENS) * SLOTS
        + lax.rem(out_row, SLOTS)
    )
    order = jnp.where(in_row == wanted, 1.0, 0.0).astype(bf16)

    def wait_tok(i, carry):
        source = lax.rem(exp + i, EXP)
        remote(
            tok_in.at[0], tok_r.at[x, source], tok_ss.at[0, i], tok_rs.at[x, source], rep, source
        ).wait_recv()
        return carry

    lax.fori_loop(1, EXP, wait_tok, 0)

    def wait_tok_x(i, carry):
        source = lax.rem(exp + i, EXP)
        remote(
            tok_in.at[0],
            tok_r.at[1 - x, source],
            tok_ss.at[1, i],
            tok_rs.at[1 - x, source],
            rep_x,
            source,
        ).wait_recv()
        return carry

    lax.fori_loop(0, EXP, wait_tok_x, 0)
    tok_local.wait()

    for side in range(2):
        rows = tok_r[side].reshape(EXP * EXPERTS_HERE * SLOTS, WIDTH)
        for piece in range(REP):
            part = dot32(order, rows[:, piece * SHARD : (piece + 1) * SHARD]).astype(bf16)
            for expert in range(EXPERTS_HERE):
                t2_s[
                    expert * 2 + piece % 2,
                    side * TOKENS : (side + 1) * TOKENS,
                    (piece // 2) * SHARD : (piece // 2 + 1) * SHARD,
                ] = part[expert * TOKENS : (expert + 1) * TOKENS]

    def t2_copy(i):
        to = lax.rem(peer + i, CHIPS)
        return remote(
            t2_s.at[to],
            t2_r.at[peer],
            t2_ss.at[i],
            t2_rs.at[peer],
            (to // 2) * 4 + x * 2 + lax.rem(to, 2),
            exp,
        )

    def start_t2(i, carry):
        t2_copy(i).start()
        return carry

    lax.fori_loop(1, CHIPS, start_t2, 0)
    t2_local = pltpu.make_async_copy(t2_s.at[peer], t2_r.at[peer], local_sem.at[3])
    t2_local.start()

    def wait_cot(i, carry):
        source = lax.rem(rep + i, REP)
        from_peer = (source // 4) * 2 + lax.rem(source, 2)
        from_x = lax.rem(source // 2, 2)
        remote(
            cot_in.at[0],
            cot_r.at[from_peer, from_x],
            cot_ss.at[i],
            cot_rs.at[source],
            source,
            exp,
        ).wait_recv()
        return carry

    lax.fori_loop(1, REP, wait_cot, 0)
    cot_local.wait()

    def wait_mom(i, carry):
        source = lax.rem(chip + i, CHIPS)
        remote(
            mom_in.at[0],
            mom_r.at[source],
            mom_ss.at[i],
            mom_rs.at[source],
            source * 2 + core,
            exp,
        ).wait_recv()
        return carry

    lax.fori_loop(1, CHIPS, wait_mom, 0)
    mom_local.wait()

    def wait_t2(i, carry):
        source = lax.rem(peer + i, CHIPS)
        remote(
            t2_s.at[0],
            t2_r.at[source],
            t2_ss.at[i],
            t2_rs.at[source],
            (source // 2) * 4 + x * 2 + lax.rem(source, 2),
            exp,
        ).wait_recv()
        return carry

    lax.fori_loop(1, CHIPS, wait_t2, 0)
    t2_local.wait()

    def new_copy(i):
        to = lax.rem(chip + i, CHIPS)
        return remote(
            new_s.at[to], new_out.at[chip], new_ss.at[i], new_rs.at[chip], to * 2 + core, exp
        )

    sq_s[...] = jnp.zeros_like(sq_s)
    cots = cot_r[...].reshape(REP * TOKENS, HIDDEN)

    def gradient(i):
        at = lax.rem(chip + i, CHIPS)
        columns = pl.ds(pl.multiple_of(at * SHARD, SHARD), SHARD)
        feats = t2_r[:, :, columns].reshape(REP * TOKENS, SHARD)
        grad = dot_rows(feats, cots)
        mom = decay_rate * mom_r[at].astype(f32) + grad
        new_s[at] = mom.astype(bf16)
        nest = (grad + decay_rate * mom).astype(bf16)
        nest_s[at] = nest
        wide = nest.astype(f32)
        squares = jnp.sum((wide * wide).reshape(SHARD // 8, 8, HIDDEN // 128, 128), axis=(0, 2))
        sq_s[...] += squares

    def gradient_send(i, carry):
        gradient(i)
        new_copy(i).start()
        return carry

    lax.fori_loop(1, CHIPS, gradient_send, 0)
    gradient(0)
    new_local = pltpu.make_async_copy(new_s.at[chip], new_out.at[chip], local_sem.at[4])
    new_local.start()

    def gram_tile(j, carry):
        columns = pl.ds(pl.multiple_of(j * TILE, TILE), TILE)
        values = nest_s[...].reshape(CHIPS * SHARD, HIDDEN)
        tile = dot_rows(values, nest_s[:, :, columns].reshape(CHIPS * SHARD, TILE))
        gram_f[:, columns] = tile
        gram_s[:, columns] = tile.astype(bf16)
        return carry

    lax.fori_loop(0, HIDDEN // TILE, gram_tile, 0)
    swap_gram = remote(gram_s, gram_r, pair_ss.at[0], pair_rs.at[0], rep_core, exp)
    swap_sq = remote(sq_s, sq_r, pair_ss.at[1], pair_rs.at[1], rep_core, exp)
    swap_gram.start()
    swap_sq.start()
    swap_sq.wait()
    swap_gram.wait()

    total = jnp.sum(jnp.sum(sq_s[...] + sq_r[...], axis=0, keepdims=True), axis=1, keepdims=True)
    inverse = 1.0 / (jnp.sqrt(total) + norm_eps)
    g0[...] = ((gram_f[...] + gram_r[...].astype(f32)) * inverse * inverse).astype(bf16)

    def tiles(body):
        def one(j, carry):
            body(pl.ds(pl.multiple_of(j * TILE, TILE), TILE))
            return carry

        lax.fori_loop(0, HIDDEN // TILE, one, 0)

    def bend0_tile(at):
        bend0[:, at] = (
            coef_b * g0[:, at].astype(f32) + coef_c * dot32(g0[...], g0[:, at])
        ).astype(bf16)

    def step_tile(at):
        step[:, at] = (
            coef_a * g0[:, at].astype(f32) + dot32(g0[...], bend0[:, at])
        ).astype(bf16)

    def g1_tile(at):
        g1[:, at] = (
            coef_a * step[:, at].astype(f32) + dot32(bend0[...], step[:, at])
        ).astype(bf16)

    def bend1_tile(at):
        bend1[:, at] = (
            coef_b * g1[:, at].astype(f32) + coef_c * dot32(g1[...], g1[:, at])
        ).astype(bf16)

    def both_tile(at):
        both[:, at] = (
            coef_a * (bend0[:, at].astype(f32) + bend1[:, at].astype(f32))
            + dot32(bend0[...], bend1[:, at])
        ).astype(bf16)

    for body in (bend0_tile, step_tile, g1_tile, bend1_tile, both_tile):
        tiles(body)

    scale = math.sqrt(WIDTH) * inverse

    def upd_copy(i):
        to = lax.rem(chip + i, CHIPS)
        return remote(
            upd_s.at[to], upd_out.at[chip], upd_ss.at[i], upd_rs.at[chip], to * 2 + core, exp
        )

    def turn(i):
        at = lax.rem(chip + i, CHIPS)
        rows = nest_s[at]
        turned = coef_a * coef_a * rows.astype(f32) + dot32(rows, both[...])
        upd_s[at] = (turned * scale).astype(bf16)

    def turn_send(i, carry):
        turn(i)
        upd_copy(i).start()
        return carry

    lax.fori_loop(1, CHIPS, turn_send, 0)
    turn(0)
    upd_local = pltpu.make_async_copy(upd_s.at[chip], upd_out.at[chip], local_sem.at[5])
    upd_local.start()

    tok_copy(0, 1).wait_send()

    def finish_tok(i, carry):
        tok_copy(i, 0).wait_send()
        tok_copy(i, 1).wait_send()
        cot_copy(i).wait_send()
        return carry

    lax.fori_loop(1, EXP, finish_tok, 0)

    def finish(i, carry):
        mom_copy(i).wait_send()
        t2_copy(i).wait_send()
        new_copy(i).wait_send()
        upd_copy(i).wait_send()
        source = lax.rem(chip + i, CHIPS)
        remote(
            new_s.at[0],
            new_out.at[source],
            new_ss.at[i],
            new_rs.at[source],
            source * 2 + core,
            exp,
        ).wait_recv()
        remote(
            upd_s.at[0],
            upd_out.at[source],
            upd_ss.at[i],
            upd_rs.at[source],
            source * 2 + core,
            exp,
        ).wait_recv()
        return carry

    lax.fori_loop(1, CHIPS, finish, 0)
    new_local.wait()
    upd_local.wait()


def on_device(acts, cotangent, counts, momentum):
    slot_count = acts.shape[3]
    slot_index = lax.broadcasted_iota(jnp.int32, (1, 1, 1, slot_count, 1), 3)
    live_rows = slot_index < counts[:, :, :, None, None]
    live = jnp.where(live_rows, acts, jnp.zeros_like(acts))
    tok = live.reshape(EXP, EXPERTS_HERE * SLOTS, WIDTH)
    cot = cotangent.reshape(CHIPS, TOKENS, HIDDEN)
    mom = momentum.transpose(1, 2, 0, 3).reshape(CHIPS, SHARD, HIDDEN)
    vmem = pltpu.VMEM
    dma = pltpu.SemaphoreType.DMA
    square = (HIDDEN, HIDDEN)
    rows = (CHIPS, SHARD, HIDDEN)
    new_rows, upd_rows = pl.pallas_call(
        kernel,
        out_shape=[jax.ShapeDtypeStruct(rows, bf16)] * 2,
        in_specs=[pl.BlockSpec(memory_space=pl.ANY)] * 3,
        out_specs=[pl.BlockSpec(memory_space=pl.ANY)] * 2,
        scratch_shapes=[
            vmem((2, EXP, EXPERTS_HERE * SLOTS, WIDTH), bf16),
            vmem((CHIPS, 2 * TOKENS, HALF), bf16),
            vmem((CHIPS, 2 * TOKENS, HALF), bf16),
            vmem((CHIPS, 2, TOKENS, HIDDEN), bf16),
            vmem(rows, bf16),
            vmem(rows, bf16),
            vmem(rows, bf16),
            vmem(rows, bf16),
            vmem(square, bf16),
            vmem(square, bf16),
            vmem(square, f32),
            vmem((8, 128), f32),
            vmem((8, 128), f32),
            vmem(square, bf16),
            vmem(square, bf16),
            vmem(square, bf16),
            vmem(square, bf16),
            vmem(square, bf16),
            vmem(square, bf16),
            dma((2, EXP)),
            dma((2, EXP)),
            dma((REP,)),
            dma((REP,)),
            dma((CHIPS,)),
            dma((CHIPS,)),
            dma((CHIPS,)),
            dma((CHIPS,)),
            dma((CHIPS,)),
            dma((CHIPS,)),
            dma((CHIPS,)),
            dma((CHIPS,)),
            dma((2,)),
            dma((2,)),
            dma((6,)),
        ],
        compiler_params=pltpu.CompilerParams(
            collective_id=0, has_side_effects=True, vmem_limit_bytes=48 << 20
        ),
        name="muon_owner",
    )(tok, cot, mom)
    shape = (EXPERTS_HERE, 2, SHARD, HIDDEN)
    new_momentum = new_rows.reshape(shape).transpose(2, 0, 1, 3)
    update = upd_rows.reshape(shape).transpose(2, 0, 1, 3)
    return (new_momentum, update)


def solution(mesh):
    in_specs = (
        P("rep", "exp", None, None, None),
        P("rep", "exp", None, None, None),
        P("rep", "exp", None),
        P("rep", "exp", None, None),
    )
    out_specs = (P("rep", "exp", None, None), P("rep", "exp", None, None))
    return jax.shard_map(
        on_device, mesh=mesh, in_specs=in_specs, out_specs=out_specs, check_vma=False
    )
```

time: 409 us -> 103 us (0.25)
  waiting for transfers between devices: 307 us -> 0 us
  Pallas kernels: 0 us -> 95.2 us
  matrix products: 28 us -> 0 us
  blocking collectives: 25.9 us -> 0 us
  starting transfers between devices: 17.5 us -> 0 us
  between operations: 15.4 us -> 0.69 us
  other arithmetic: 9 us -> 2.42 us
    reduce_scatter x1 -> x0, waiting for transfers between devices: 265 us -> none  [on_device(): lax.psum_scatter(jnp.einsum('secd,ekscf->dekf', feature_cols, grads_out,...]
    pallas_call x0 -> x1, Pallas kernels: none -> 95.2 us  [on_device(): pl.pallas_call(kernel, out_shape=[jax.ShapeDtypeStruct(rows, bf16)] * 2,...]
    all_to_all x2 -> x0, waiting for transfers between devices: 35.7 us -> none  [the longest x1 18.8 us: on_device(): lax.all_to_all(ortho.reshape(replicas, pieces, hidden), 'rep', split_axis...]
    dot_general x5 -> x0, matrix products: 28 us -> none  [the longest x1 11.7 us: on_device(): jnp.einsum('secd,ekscf->dekf', feature_cols, grads_out, preferred_element...]
    all_to_all x1 -> x0, blocking collectives: 25.9 us -> none  [on_device(): lax.all_to_all(send_rows, 'rep', split_axis=0, concat_axis=0, tiled=True)]
    all_to_all x2 -> x0, starting transfers between devices: 15.3 us -> none  [the longest x1 11.6 us: on_device(): lax.all_to_all(live, 'exp', split_axis=2, concat_axis=1, tiled=True)]
    ppermute x3 -> x0, waiting for transfers between devices: 6.09 us -> none  [swapped(): return lax.ppermute(value, axis, pairs)]
    unnamed x10 -> x4, local copies, waits for them, and re-layouts: 6.08 us -> 0.7 us
  transfers between devices with their start and end apart: 6 -> 0, of which waited for: 6 -> 0; matrix products, arithmetic and copies ran while one was open for 1% -> 0% of each run, Pallas kernels for 0% -> 0%
where the time goes in v1:
time: 103 us
  Pallas kernels  95.2 us (92%)
  local copies, waits for them, and re-layouts  4.76 us (5%)
  other arithmetic  2.42 us (2%)
    pallas_call x1, Pallas kernels, on_device(): pl.pallas_call(kernel, out_shape=[jax.ShapeDtypeStruct(rows, bf16)] * 2,...  95.2 us
    transpose x1, local copies, waits for them, and re-layouts, on_device(): update = upd_rows.reshape(shape).transpose(2, 0, 1, 3)  3.58 us

profile of v1, /device:TPU:1, one launch (start us, length us, event | category | flops | bytes accessed | tf_op | source)
XLA Modules:
  0.0 103.0 jit_solution(8392340259151361440)
XLA Ops:
  0.6 0.0 copy-start.1
  0.6 0.8 iota_compare_fusion
  1.5 1.6 %broadcast_select_fusion = bf16[1,1,64,2,2048]{4,3,2,1,0:T(2,128)(2,1)S(1)} fusion(bf16[1,1,64,2,2048]{4,3,2,1,0:T(2,128)(2,1)} %param.4, pred[64,2]{1,0:T(8,128)(4,1)S(1)} %iota_compare_fusion), kind=kLoop, calls=%fused_computation.2 | loop fusion | flops 262144 | bytes 1048704 | tf_op jit(solution)/shard_map/jit(_where)/select_n | solution.py:435
  3.1 0.2 reshape.48.tok_in
  3.3 0.0 copy-done.1
  3.3 0.0 copy-start
  3.3 0.3 copy.6
  3.6 0.7 copy-done
  4.3 95.2 %muon_owner.1 = (bf16[8,128,768]{2,1,0:T(8,128)(2,1)S(1)}, bf16[8,128,768]{2,1,0:T(8,128)(2,1)S(1)}) custom-call(bf16[16,8,2048]{2,1,0:T(8,128)(2,1)S(1)} %reshape.48.tok_in, bf16[8,32,768]{2,1,0:T(8,128)(2,1)S(1)} %bitcast.13, bf16[8,128,768]{2,1,0:T(8,128)(2,1)S(1)} %bitcast.10), custom_call_target="tpu_custom_call" | custom-call | tf_op jit(solution)/shard_map/muon_owner/pallas_call | solution.py:443
  99.5 3.6 %copy_bitcast_fusion = (bf16[128,4,2,768]{3,2,1,0:T(2,128)(2,1)}, bf16[128,4,2,768]{3,2,1,0:T(2,128)(2,1)}) fusion(bf16[4,2,128,768]{3,2,1,0:T(8,128)(2,1)S(1)} %bitcast.12, bf16[4,2,128,768]{3,2,1,0:T(8,128)(2,1)S(1)} %bitcast.11), kind=kLoop, calls=%fused_computation | loop fusion | bytes 6291456 | tf_op jit(solution)/shard_map/transpose | solution.py:491
Async XLA Ops:
  0.6 2.7 %copy-start.1 = (bf16[128,4,2,768]{3,2,1,0:T(2,128)(2,1)S(1)}, bf16[128,4,2,768]{3,2,1,0:T(2,128)(2,1)}, u32[]{:S(2)}) copy-start(bf16[128,4,2,768]{3,2,1,0:T(2,128)(2,1)} %param.7) | copy-start | bytes 4718596
  3.3 1.0 copy-start

commit v2 on v1

--- a/solution.py
+++ b/solution.py
@@ -19,7 +19,10 @@
 CHIPS = 8
 YS = 4
 EXPERTS_HERE = 4
+SIDES = 2
+SIDE_EXPERTS = EXPERTS_HERE // SIDES
 SLOTS = 2
+SIDE_ROWS = SIDE_EXPERTS * SLOTS
 WIDTH = 2048
 HALF = WIDTH // 2
 SHARD = 128
@@ -52,11 +55,13 @@
 
 
 def kernel(
-    tok_in,
+    counts,
+    acts_in,
     cot_in,
     mom_in,
     new_out,
     upd_out,
+    tok_in,
     tok_r,
     t2_s,
     t2_r,
@@ -80,6 +85,7 @@
     tok_rs,
     cot_ss,
     cot_rs,
+    fwd_ss,
     mom_ss,
     mom_rs,
     t2_ss,
@@ -101,6 +107,10 @@
     peer = y * 2 + core
     rep_x = y * 4 + (1 - x) * 2 + core
     rep_core = chip * 2 + (1 - core)
+    mine = 4 * x + y
+
+    def matrix(of_chip):
+        return 4 * lax.rem(of_chip, 2) + of_chip // 2
 
     def signal(to_rep, to_exp):
         pl.semaphore_signal(
@@ -114,12 +124,25 @@
         return carry
 
     lax.fori_loop(1, 16, greet, 0)
+
+    row = lax.broadcasted_iota(jnp.int32, (SIDE_ROWS, WIDTH), 0)
+
+    def mask(i, carry):
+        group = i // SIDES
+        side = lax.rem(i, SIDES)
+        at = i * SIDE_EXPERTS
+        count = jnp.where(row < SLOTS, counts[at], counts[at + 1])
+        values = acts_in[group, side].astype(f32)
+        tok_in[group, side] = jnp.where(lax.rem(row, SLOTS) < count, values, 0.0).astype(bf16)
+        return carry
+
+    lax.fori_loop(0, EXP * SIDES, mask, 0)
     pl.semaphore_wait(pltpu.get_barrier_semaphore(), 45)
 
     def tok_copy(i, other):
         to = lax.rem(exp + i, EXP)
         return remote(
-            tok_in.at[to],
+            tok_in.at[to, 1 - x if other else x],
             tok_r.at[x, exp],
             tok_ss.at[other, i],
             tok_rs.at[x, exp],
@@ -128,20 +151,30 @@
         )
 
     def cot_copy(i):
-        to = lax.rem(rep + i, REP)
-        return remote(
-            cot_in.at[to // 2], cot_r.at[peer, x], cot_ss.at[i], cot_rs.at[rep], to, exp
+        to = lax.rem(chip + i, CHIPS)
+        return remote(
+            cot_in.at[matrix(to)],
+            cot_r.at[peer, x],
+            cot_ss.at[i],
+            cot_rs.at[peer, x],
+            to * 2 + core,
+            exp,
         )
 
     def mom_copy(i):
         to = lax.rem(chip + i, CHIPS)
         return remote(
-            mom_in.at[to], mom_r.at[chip], mom_ss.at[i], mom_rs.at[chip], to * 2 + core, exp
-        )
-
-    tok_local = pltpu.make_async_copy(tok_in.at[exp], tok_r.at[x, exp], local_sem.at[0])
-    cot_local = pltpu.make_async_copy(cot_in.at[chip], cot_r.at[peer, x], local_sem.at[1])
-    mom_local = pltpu.make_async_copy(mom_in.at[chip], mom_r.at[chip], local_sem.at[2])
+            mom_in.at[matrix(to)],
+            mom_r.at[chip],
+            mom_ss.at[i],
+            mom_rs.at[chip],
+            to * 2 + core,
+            exp,
+        )
+
+    tok_local = pltpu.make_async_copy(tok_in.at[exp, x], tok_r.at[x, exp], local_sem.at[0])
+    cot_local = pltpu.make_async_copy(cot_in.at[mine], cot_r.at[peer, x], local_sem.at[1])
+    mom_local = pltpu.make_async_copy(mom_in.at[mine], mom_r.at[chip], local_sem.at[2])
 
     tok_copy(0, 1).start()
 
@@ -156,7 +189,7 @@
         cot_copy(i).start()
         return carry
 
-    lax.fori_loop(1, REP, start_cot, 0)
+    lax.fori_loop(1, CHIPS, start_cot, 0)
 
     def start_mom(i, carry):
         mom_copy(i).start()
@@ -170,8 +203,8 @@
     out_row = lax.broadcasted_iota(jnp.int32, (SHARD, SHARD), 0)
     in_row = lax.broadcasted_iota(jnp.int32, (SHARD, SHARD), 1)
     wanted = (
-        lax.rem(out_row // SLOTS, EXP) * (EXPERTS_HERE * SLOTS)
-        + (out_row // TOKENS) * SLOTS
+        lax.rem(out_row // SLOTS, SIDES * EXP) * SIDE_ROWS
+        + (out_row // (SIDES * TOKENS)) * SLOTS
         + lax.rem(out_row, SLOTS)
     )
     order = jnp.where(in_row == wanted, 1.0, 0.0).astype(bf16)
@@ -179,7 +212,7 @@
     def wait_tok(i, carry):
         source = lax.rem(exp + i, EXP)
         remote(
-            tok_in.at[0], tok_r.at[x, source], tok_ss.at[0, i], tok_rs.at[x, source], rep, source
+            tok_in.at[0, 0], tok_r.at[x, source], tok_ss.at[0, i], tok_rs.at[x, source], rep, source
         ).wait_recv()
         return carry
 
@@ -188,7 +221,7 @@
     def wait_tok_x(i, carry):
         source = lax.rem(exp + i, EXP)
         remote(
-            tok_in.at[0],
+            tok_in.at[0, 0],
             tok_r.at[1 - x, source],
             tok_ss.at[1, i],
             tok_rs.at[1 - x, source],
@@ -200,21 +233,18 @@
     lax.fori_loop(0, EXP, wait_tok_x, 0)
     tok_local.wait()
 
-    for side in range(2):
-        rows = tok_r[side].reshape(EXP * EXPERTS_HERE * SLOTS, WIDTH)
-        for piece in range(REP):
-            part = dot32(order, rows[:, piece * SHARD : (piece + 1) * SHARD]).astype(bf16)
-            for expert in range(EXPERTS_HERE):
-                t2_s[
-                    expert * 2 + piece % 2,
-                    side * TOKENS : (side + 1) * TOKENS,
-                    (piece // 2) * SHARD : (piece // 2 + 1) * SHARD,
-                ] = part[expert * TOKENS : (expert + 1) * TOKENS]
+    rows = tok_r[...].reshape(SIDES * EXP * SIDE_ROWS, WIDTH)
+    for piece in range(REP):
+        part = dot32(order, rows[:, piece * SHARD : (piece + 1) * SHARD]).astype(bf16)
+        for expert in range(SIDE_EXPERTS):
+            t2_s[expert, piece % 2, :, (piece // 2) * SHARD : (piece // 2 + 1) * SHARD] = part[
+                expert * SIDES * TOKENS : (expert + 1) * SIDES * TOKENS
+            ]
 
     def t2_copy(i):
         to = lax.rem(peer + i, CHIPS)
         return remote(
-            t2_s.at[to],
+            t2_s.at[to // 4, lax.rem(to, 2)],
             t2_r.at[peer],
             t2_ss.at[i],
             t2_rs.at[peer],
@@ -227,40 +257,64 @@
         return carry
 
     lax.fori_loop(1, CHIPS, start_t2, 0)
-    t2_local = pltpu.make_async_copy(t2_s.at[peer], t2_r.at[peer], local_sem.at[3])
+    t2_local = pltpu.make_async_copy(t2_s.at[y // 2, core], t2_r.at[peer], local_sem.at[3])
     t2_local.start()
 
+    def forward(of_chip):
+        at = (of_chip // 2) * 2 + core
+        side = lax.rem(of_chip, 2)
+        return remote(
+            cot_r.at[at, side],
+            cot_r.at[at, side],
+            fwd_ss.at[of_chip],
+            cot_rs.at[at, side],
+            rep_core,
+            exp,
+        )
+
     def wait_cot(i, carry):
-        source = lax.rem(rep + i, REP)
-        from_peer = (source // 4) * 2 + lax.rem(source, 2)
-        from_x = lax.rem(source // 2, 2)
+        source = lax.rem(chip + i, CHIPS)
+        at = (source // 2) * 2 + core
+        side = lax.rem(source, 2)
         remote(
             cot_in.at[0],
-            cot_r.at[from_peer, from_x],
+            cot_r.at[at, side],
             cot_ss.at[i],
-            cot_rs.at[source],
-            source,
-            exp,
-        ).wait_recv()
-        return carry
-
-    lax.fori_loop(1, REP, wait_cot, 0)
+            cot_rs.at[at, side],
+            source * 2 + core,
+            exp,
+        ).wait_recv()
+        forward(source).start()
+        return carry
+
     cot_local.wait()
-
-    def wait_mom(i, carry):
-        source = lax.rem(chip + i, CHIPS)
+    forward(chip).start()
+    lax.fori_loop(1, CHIPS, wait_cot, 0)
+
+    def wait_forward(i, carry):
+        at = (i // 2) * 2 + 1 - core
+        side = lax.rem(i, 2)
+        remote(
+            cot_r.at[at, side],
+            cot_r.at[at, side],
+            fwd_ss.at[i],
+            cot_rs.at[at, side],
+            rep_core,
+            exp,
+        ).wait_recv()
+        return carry
+
+    lax.fori_loop(0, CHIPS, wait_forward, 0)
+
+    def wait_mom(source):
         remote(
             mom_in.at[0],
             mom_r.at[source],
-            mom_ss.at[i],
+            mom_ss.at[0],
             mom_rs.at[source],
             source * 2 + core,
             exp,
         ).wait_recv()
-        return carry
-
-    lax.fori_loop(1, CHIPS, wait_mom, 0)
-    mom_local.wait()
 
     def wait_t2(i, carry):
         source = lax.rem(peer + i, CHIPS)
@@ -280,7 +334,7 @@
     def new_copy(i):
         to = lax.rem(chip + i, CHIPS)
         return remote(
-            new_s.at[to], new_out.at[chip], new_ss.at[i], new_rs.at[chip], to * 2 + core, exp
+            new_s.at[to], new_out.at[mine], new_ss.at[i], new_rs.at[chip], to * 2 + core, exp
         )
 
     sq_s[...] = jnp.zeros_like(sq_s)
@@ -300,13 +354,15 @@
         sq_s[...] += squares
 
     def gradient_send(i, carry):
+        wait_mom(lax.rem(chip + i, CHIPS))
         gradient(i)
         new_copy(i).start()
         return carry
 
     lax.fori_loop(1, CHIPS, gradient_send, 0)
+    mom_local.wait()
     gradient(0)
-    new_local = pltpu.make_async_copy(new_s.at[chip], new_out.at[chip], local_sem.at[4])
+    new_local = pltpu.make_async_copy(new_s.at[chip], new_out.at[mine], local_sem.at[4])
     new_local.start()
 
     def gram_tile(j, carry):
@@ -370,7 +426,7 @@
     def upd_copy(i):
         to = lax.rem(chip + i, CHIPS)
         return remote(
-            upd_s.at[to], upd_out.at[chip], upd_ss.at[i], upd_rs.at[chip], to * 2 + core, exp
+            upd_s.at[to], upd_out.at[mine], upd_ss.at[i], upd_rs.at[chip], to * 2 + core, exp
         )
 
     def turn(i):
@@ -386,7 +442,7 @@
 
     lax.fori_loop(1, CHIPS, turn_send, 0)
     turn(0)
-    upd_local = pltpu.make_async_copy(upd_s.at[chip], upd_out.at[chip], local_sem.at[5])
+    upd_local = pltpu.make_async_copy(upd_s.at[chip], upd_out.at[mine], local_sem.at[5])
     upd_local.start()
 
     tok_copy(0, 1).wait_send()
@@ -394,12 +450,15 @@
     def finish_tok(i, carry):
         tok_copy(i, 0).wait_send()
         tok_copy(i, 1).wait_send()
+        return carry
+
+    lax.fori_loop(1, EXP, finish_tok, 0)
+
+    forward(chip).wait_send()
+
+    def finish(i, carry):
         cot_copy(i).wait_send()
-        return carry
-
-    lax.fori_loop(1, EXP, finish_tok, 0)
-
-    def finish(i, carry):
+        forward(lax.rem(chip + i, CHIPS)).wait_send()
         mom_copy(i).wait_send()
         t2_copy(i).wait_send()
         new_copy(i).wait_send()
@@ -407,7 +466,7 @@
         source = lax.rem(chip + i, CHIPS)
         remote(
             new_s.at[0],
-            new_out.at[source],
+            new_out.at[matrix(source)],
             new_ss.at[i],
             new_rs.at[source],
             source * 2 + core,
@@ -415,7 +474,7 @@
         ).wait_recv()
         remote(
             upd_s.at[0],
-            upd_out.at[source],
+            upd_out.at[matrix(source)],
             upd_ss.at[i],
             upd_rs.at[source],
             source * 2 + core,
@@ -429,11 +488,8 @@
 
 
 def on_device(acts, cotangent, counts, momentum):
-    slot_count = acts.shape[3]
-    slot_index = lax.broadcasted_iota(jnp.int32, (1, 1, 1, slot_count, 1), 3)
-    live_rows = slot_index < counts[:, :, :, None, None]
-    live = jnp.where(live_rows, acts, jnp.zeros_like(acts))
-    tok = live.reshape(EXP, EXPERTS_HERE * SLOTS, WIDTH)
+    live = counts.reshape(EXP * EXPERTS_HERE)
+    tok = acts.reshape(EXP, SIDES, SIDE_ROWS, WIDTH)
     cot = cotangent.reshape(CHIPS, TOKENS, HIDDEN)
     mom = momentum.transpose(1, 2, 0, 3).reshape(CHIPS, SHARD, HIDDEN)
     vmem = pltpu.VMEM
@@ -443,11 +499,17 @@
     new_rows, upd_rows = pl.pallas_call(
         kernel,
         out_shape=[jax.ShapeDtypeStruct(rows, bf16)] * 2,
-        in_specs=[pl.BlockSpec(memory_space=pl.ANY)] * 3,
+        in_specs=[
+            pl.BlockSpec(memory_space=pltpu.SMEM),
+            pl.BlockSpec(memory_space=pltpu.VMEM),
+            pl.BlockSpec(memory_space=pl.ANY),
+            pl.BlockSpec(memory_space=pl.ANY),
+        ],
         out_specs=[pl.BlockSpec(memory_space=pl.ANY)] * 2,
         scratch_shapes=[
-            vmem((2, EXP, EXPERTS_HERE * SLOTS, WIDTH), bf16),
-            vmem((CHIPS, 2 * TOKENS, HALF), bf16),
+            vmem((EXP, SIDES, SIDE_ROWS, WIDTH), bf16),
+            vmem((SIDES, EXP, SIDE_ROWS, WIDTH), bf16),
+            vmem((SIDE_EXPERTS, 2, SIDES * TOKENS, HALF), bf16),
             vmem((CHIPS, 2 * TOKENS, HALF), bf16),
             vmem((CHIPS, 2, TOKENS, HIDDEN), bf16),
             vmem(rows, bf16),
@@ -467,8 +529,9 @@
             vmem(square, bf16),
             dma((2, EXP)),
             dma((2, EXP)),
-            dma((REP,)),
-            dma((REP,)),
+            dma((CHIPS,)),
+            dma((CHIPS, SIDES)),
+            dma((CHIPS,)),
             dma((CHIPS,)),
             dma((CHIPS,)),
             dma((CHIPS,)),
@@ -485,7 +548,7 @@
             collective_id=0, has_side_effects=True, vmem_limit_bytes=48 << 20
         ),
         name="muon_owner",
-    )(tok, cot, mom)
+    )(live, tok, cot, mom)
     shape = (EXPERTS_HERE, 2, SHARD, HIDDEN)
     new_momentum = new_rows.reshape(shape).transpose(2, 0, 1, 3)
     update = upd_rows.reshape(shape).transpose(2, 0, 1, 3)

time: 103 us -> 93.3 us (0.906)
  Pallas kernels: 95.2 us -> 85.1 us
  local copies, waits for them, and re-layouts: 4.76 us -> 7.34 us
  other arithmetic: 2.42 us -> 0 us
    pallas_call x1, Pallas kernels: 95.2 us -> 85.1 us  [on_device(): pl.pallas_call(kernel, out_shape=[jax.ShapeDtypeStruct(rows, bf16)] * 2,...]
    reshape x1, local copies, waits for them, and re-layouts: 0.2 us -> 2 us  [on_device(): tok = acts.reshape(EXP, SIDES, SIDE_ROWS, WIDTH)]
    select_n x1 -> x0, other arithmetic: 1.58 us -> none  [on_device(): live = jnp.where(live_rows, acts, jnp.zeros_like(acts))]
    transpose x1, local copies, waits for them, and re-layouts: 0.29 us -> 1.75 us  [on_device(): mom = momentum.transpose(1, 2, 0, 3).reshape(CHIPS, SHARD, HIDDEN)]
where the time goes in v2:
time: 93.3 us; the launch traced here: 93.2 us
  Pallas kernels  85.1 us (91%)
  local copies, waits for them, and re-layouts  7.34 us (8%)
    pallas_call x1, Pallas kernels, on_device(): pl.pallas_call(kernel, out_shape=[jax.ShapeDtypeStruct(rows, bf16)] * 2,...  85.1 us
    transpose x1, local copies, waits for them, and re-layouts, on_device(): update = upd_rows.reshape(shape).transpose(2, 0, 1, 3)  3.58 us
    reshape x1, local copies, waits for them, and re-layouts, on_device(): tok = acts.reshape(EXP, SIDES, SIDE_ROWS, WIDTH)  2 us

profile of v2, /device:TPU:1, one launch (start us, length us, event | category | flops | bytes accessed | tf_op | source)
XLA Modules:
  0.0 93.2 jit_solution(3611212897854052723)
XLA Ops:
  0.6 2.0 %reshape.23.acts_in = bf16[16,2,4,2048]{3,2,1,0:T(4,128)(2,1)S(1)} reshape(bf16[1,1,64,2,2048]{4,3,2,1,0:T(2,128)(2,1)} %param.4) | data formatting | bytes 1048576 | tf_op jit(solution)/shard_map/reshape | solution.py:492
  2.6 0.0 copy-start
  2.7 0.0 copy-start.1
  2.7 1.7 %copy.6 = bf16[4,2,128,768]{3,2,1,0:T(8,128)(2,1)S(1)} copy(bf16[4,2,128,768]{3,1,0,2:T(2,128)(2,1)} %bitcast.15) | data formatting | bytes 3145728 | tf_op jit(solution)/shard_map/transpose | solution.py:494
  4.4 0.0 copy-done
  4.4 0.0 copy-done.1
  4.4 85.1 %muon_owner.1 = (bf16[8,128,768]{2,1,0:T(8,128)(2,1)S(1)}, bf16[8,128,768]{2,1,0:T(8,128)(2,1)S(1)}) custom-call(s32[64]{0:T(128)S(1)} %bitcast.14, bf16[16,2,4,2048]{3,2,1,0:T(4,128)(2,1)S(1)} %reshape.23.acts_in, bf16[8,32,768]{2,1,0:T(8,128)(2,1)S(1)} %bitcast.13, bf16[8,128,768]{2,1,0:T(8,128)(2,1)S(1)} %bitcast.10), custom_call_target="tpu_custom_call" | custom-call | tf_op jit(solution)/shard_map/muon_owner/pallas_call | solution.py:499
  89.6 3.6 %copy_bitcast_fusion = (bf16[128,4,2,768]{3,2,1,0:T(2,128)(2,1)}, bf16[128,4,2,768]{3,2,1,0:T(2,128)(2,1)}) fusion(bf16[4,2,128,768]{3,2,1,0:T(8,128)(2,1)S(1)} %bitcast.12, bf16[4,2,128,768]{3,2,1,0:T(8,128)(2,1)S(1)} %bitcast.11), kind=kLoop, calls=%fused_computation | loop fusion | bytes 6291456 | tf_op jit(solution)/shard_map/transpose | solution.py:554
Async XLA Ops:
  2.6 1.8 %copy-start = (bf16[1,4,2,32,768]{4,3,2,1,0:T(8,128)(2,1)S(1)}, bf16[1,4,2,32,768]{4,3,2,1,0:T(8,128)(2,1)}, u32[]{:S(2)}) copy-start(bf16[1,4,2,32,768]{4,3,2,1,0:T(8,128)(2,1)} %param.5) | copy-start | bytes 1179652
  2.7 1.8 %copy-start.1 = (s32[1,1,64]{2,1,0:T(1,128)S(1)}, s32[1,1,64]{2,1,0:T(1,128)}, u32[]{:S(2)}) copy-start(s32[1,1,64]{2,1,0:T(1,128)} %param.6) | copy-start | bytes 772

commit v3 on v2

--- a/solution.py
+++ b/solution.py
@@ -56,11 +56,18 @@
 
 def kernel(
     counts,
+    acts_hbm,
+    cot_in,
+    mom_hbm,
+    new_hbm,
+    upd_hbm,
     acts_in,
-    cot_in,
+    mom_raw,
     mom_in,
     new_out,
     upd_out,
+    new_mix,
+    upd_mix,
     tok_in,
     tok_r,
     t2_s,
@@ -124,6 +131,10 @@
         return carry
 
     lax.fori_loop(1, 16, greet, 0)
+    acts_load = pltpu.make_async_copy(acts_hbm, acts_in, local_sem.at[6])
+    mom_load = pltpu.make_async_copy(mom_hbm, mom_raw, local_sem.at[7])
+    acts_load.start()
+    mom_load.start()
 
     row = lax.broadcasted_iota(jnp.int32, (SIDE_ROWS, WIDTH), 0)
 
@@ -132,10 +143,11 @@
         side = lax.rem(i, SIDES)
         at = i * SIDE_EXPERTS
         count = jnp.where(row < SLOTS, counts[at], counts[at + 1])
-        values = acts_in[group, side].astype(f32)
+        values = acts_in[pl.ds(at, SIDE_EXPERTS)].astype(f32).reshape(SIDE_ROWS, WIDTH)
         tok_in[group, side] = jnp.where(lax.rem(row, SLOTS) < count, values, 0.0).astype(bf16)
         return carry
 
+    acts_load.wait()
     lax.fori_loop(0, EXP * SIDES, mask, 0)
     pl.semaphore_wait(pltpu.get_barrier_semaphore(), 45)
 
@@ -191,6 +203,10 @@
 
     lax.fori_loop(1, CHIPS, start_cot, 0)
 
+    mom_load.wait()
+    for expert in range(EXPERTS_HERE):
+        mom_in[2 * expert : 2 * expert + 2] = jnp.swapaxes(mom_raw[:, expert], 0, 1)
+
     def start_mom(i, carry):
         mom_copy(i).start()
         return carry
@@ -334,7 +350,7 @@
     def new_copy(i):
         to = lax.rem(chip + i, CHIPS)
         return remote(
-            new_s.at[to], new_out.at[mine], new_ss.at[i], new_rs.at[chip], to * 2 + core, exp
+            new_s.at[to], new_out.at[mine], new_ss.at[i], new_rs.at[mine], to * 2 + core, exp
         )
 
     sq_s[...] = jnp.zeros_like(sq_s)
@@ -426,7 +442,7 @@
     def upd_copy(i):
         to = lax.rem(chip + i, CHIPS)
         return remote(
-            upd_s.at[to], upd_out.at[mine], upd_ss.at[i], upd_rs.at[chip], to * 2 + core, exp
+            upd_s.at[to], upd_out.at[mine], upd_ss.at[i], upd_rs.at[mine], to * 2 + core, exp
         )
 
     def turn(i):
@@ -444,6 +460,40 @@
     turn(0)
     upd_local = pltpu.make_async_copy(upd_s.at[chip], upd_out.at[mine], local_sem.at[5])
     upd_local.start()
+
+    def wait_new(i, carry):
+        source = lax.rem(chip + i, CHIPS)
+        remote(
+            new_s.at[0],
+            new_out.at[matrix(source)],
+            new_ss.at[i],
+            new_rs.at[matrix(source)],
+            source * 2 + core,
+            exp,
+        ).wait_recv()
+        return carry
+
+    lax.fori_loop(1, CHIPS, wait_new, 0)
+    new_local.wait()
+
+    mix = jnp.where(
+        out_row == lax.rem(in_row, SHARD // 2) * 2 + in_row // (SHARD // 2), 1.0, 0.0
+    ).astype(bf16)
+
+    def interleave(source, target, expert):
+        for part in range(2):
+            half = slice(part * (SHARD // 2), (part + 1) * (SHARD // 2))
+            pair = jnp.concatenate(
+                [source[2 * expert, half], source[2 * expert + 1, half]], axis=0
+            )
+            target[half, expert] = (
+                dot32(mix, pair).astype(bf16).reshape(SHARD // 2, 2, HIDDEN)
+            )
+
+    for expert in range(EXPERTS_HERE):
+        interleave(new_out, new_mix, expert)
+    new_store = pltpu.make_async_copy(new_mix, new_hbm, local_sem.at[8])
+    new_store.start()
 
     tok_copy(0, 1).wait_send()
 
@@ -462,51 +512,65 @@
         mom_copy(i).wait_send()
         t2_copy(i).wait_send()
         new_copy(i).wait_send()
-        upd_copy(i).wait_send()
+        return carry
+
+    lax.fori_loop(1, CHIPS, finish, 0)
+    upd_local.wait()
+
+    def wait_upd(i, carry):
         source = lax.rem(chip + i, CHIPS)
-        remote(
-            new_s.at[0],
-            new_out.at[matrix(source)],
-            new_ss.at[i],
-            new_rs.at[source],
-            source * 2 + core,
-            exp,
-        ).wait_recv()
         remote(
             upd_s.at[0],
             upd_out.at[matrix(source)],
             upd_ss.at[i],
-            upd_rs.at[source],
+            upd_rs.at[matrix(source)],
             source * 2 + core,
             exp,
         ).wait_recv()
         return carry
 
-    lax.fori_loop(1, CHIPS, finish, 0)
-    new_local.wait()
-    upd_local.wait()
+    lax.fori_loop(1, CHIPS, wait_upd, 0)
+    for expert in range(EXPERTS_HERE):
+        interleave(upd_out, upd_mix, expert)
+    upd_store = pltpu.make_async_copy(upd_mix, upd_hbm, local_sem.at[9])
+    upd_store.start()
+
+    def finish_upd(i, carry):
+        upd_copy(i).wait_send()
+        return carry
+
+    lax.fori_loop(1, CHIPS, finish_upd, 0)
+    new_store.wait()
+    upd_store.wait()
 
 
 def on_device(acts, cotangent, counts, momentum):
     live = counts.reshape(EXP * EXPERTS_HERE)
-    tok = acts.reshape(EXP, SIDES, SIDE_ROWS, WIDTH)
+    tok = acts.reshape(EXP * EXPERTS_HERE, SLOTS, WIDTH)
     cot = cotangent.reshape(CHIPS, TOKENS, HIDDEN)
-    mom = momentum.transpose(1, 2, 0, 3).reshape(CHIPS, SHARD, HIDDEN)
     vmem = pltpu.VMEM
     dma = pltpu.SemaphoreType.DMA
     square = (HIDDEN, HIDDEN)
     rows = (CHIPS, SHARD, HIDDEN)
-    new_rows, upd_rows = pl.pallas_call(
+    mixed = (SHARD, EXPERTS_HERE, 2, HIDDEN)
+    return pl.pallas_call(
         kernel,
-        out_shape=[jax.ShapeDtypeStruct(rows, bf16)] * 2,
+        out_shape=(jax.ShapeDtypeStruct(mixed, bf16),) * 2,
         in_specs=[
             pl.BlockSpec(memory_space=pltpu.SMEM),
-            pl.BlockSpec(memory_space=pltpu.VMEM),
+            pl.BlockSpec(memory_space=pl.ANY),
             pl.BlockSpec(memory_space=pl.ANY),
             pl.BlockSpec(memory_space=pl.ANY),
         ],
-        out_specs=[pl.BlockSpec(memory_space=pl.ANY)] * 2,
+        out_specs=(pl.BlockSpec(memory_space=pl.ANY),) * 2,
         scratch_shapes=[
+            vmem((EXP * EXPERTS_HERE, SLOTS, WIDTH), bf16),
+            vmem(mixed, bf16),
+            vmem(rows, bf16),
+            vmem(rows, bf16),
+            vmem(rows, bf16),
+            vmem(mixed, bf16),
+            vmem(mixed, bf16),
             vmem((EXP, SIDES, SIDE_ROWS, WIDTH), bf16),
             vmem((SIDES, EXP, SIDE_ROWS, WIDTH), bf16),
             vmem((SIDE_EXPERTS, 2, SIDES * TOKENS, HALF), bf16),
@@ -542,17 +606,13 @@
             dma((CHIPS,)),
             dma((2,)),
             dma((2,)),
-            dma((6,)),
+            dma((10,)),
         ],
         compiler_params=pltpu.CompilerParams(
-            collective_id=0, has_side_effects=True, vmem_limit_bytes=48 << 20
+            collective_id=0, has_side_effects=True, vmem_limit_bytes=60 << 20
         ),
         name="muon_owner",
-    )(live, tok, cot, mom)
-    shape = (EXPERTS_HERE, 2, SHARD, HIDDEN)
-    new_momentum = new_rows.reshape(shape).transpose(2, 0, 1, 3)
-    update = upd_rows.reshape(shape).transpose(2, 0, 1, 3)
-    return (new_momentum, update)
+    )(live, tok, cot, momentum)
 
 
 def solution(mesh):

time: 93.3 us -> 92.8 us (level)
  local copies, waits for them, and re-layouts: 7.34 us -> 4.89 us
  Pallas kernels: 85.1 us -> 87.1 us
    transpose x2 -> x0, local copies, waits for them, and re-layouts: 5.33 us -> none  [the longest x1 3.58 us: on_device(): update = upd_rows.reshape(shape).transpose(2, 0, 1, 3)]
    unnamed x4, local copies, waits for them, and re-layouts: 0.01 us -> 4.89 us
    reshape x1 -> x0, local copies, waits for them, and re-layouts: 2 us -> none  [on_device(): tok = acts.reshape(EXP, SIDES, SIDE_ROWS, WIDTH)]
    pallas_call x1, Pallas kernels: 85.1 us -> 87.1 us  [on_device(): pl.pallas_call(kernel, out_shape=(jax.ShapeDtypeStruct(mixed, bf16),) * 2...]
where the time goes in v3:
time: 92.8 us; the launch traced here: 92.7 us
  Pallas kernels  87.1 us (94%)
  local copies, waits for them, and re-layouts  4.89 us (5%)
    pallas_call x1, Pallas kernels, on_device(): pl.pallas_call(kernel, out_shape=(jax.ShapeDtypeStruct(mixed, bf16),) * 2...  87.1 us
    unnamed x4, local copies, waits for them, and re-layouts  4.89 us

profile of v3, /device:TPU:1, one launch (start us, length us, event | category | flops | bytes accessed | tf_op | source)
XLA Modules:
  0.0 92.7 jit_solution(1929669655065089797)
XLA Ops:
  0.6 87.1 %muon_owner.1 = (bf16[128,4,2,768]{3,2,1,0:T(2,128)(2,1)}, bf16[128,4,2,768]{3,2,1,0:T(2,128)(2,1)}) custom-call(s32[64]{0:T(128)} %bitcast.5, bf16[64,2,2048]{2,1,0:T(2,128)(2,1)} %bitcast.3, bf16[8,32,768]{2,1,0:T(8,128)(2,1)} %bitcast.4, bf16[128,4,2,768]{3,2,1,0:T(2,128)(2,1)} %mom_hbm.1), custom_call_target="tpu_custom_call" | custom-call | tf_op jit(solution)/shard_map/muon_owner/pallas_call | solution.py:556
  87.8 0.0 copy-start
  87.8 3.7 %copy.8 = bf16[128,4,2,768]{3,2,1,0:T(2,128)(2,1)} copy(bf16[128,4,2,768]{3,2,1,0:T(2,128)(2,1)} %get-tuple-element.4) | data formatting | bytes 3145728
  91.5 0.0 copy-done
  91.5 1.1 %copy.9 = bf16[128,4,2,768]{3,2,1,0:T(2,128)(2,1)} copy(bf16[128,4,2,768]{3,2,1,0:T(2,128)(2,1)S(1)} %copy-done) | data formatting | bytes 3145728
Async XLA Ops:
  87.8 3.8 %copy-start = (bf16[128,4,2,768]{3,2,1,0:T(2,128)(2,1)S(1)}, bf16[128,4,2,768]{3,2,1,0:T(2,128)(2,1)}, u32[]{:S(2)}) copy-start(bf16[128,4,2,768]{3,2,1,0:T(2,128)(2,1)} %get-tuple-element.5) | copy-start | bytes 4718596

commit v4 on v3

--- a/solution.py
+++ b/solution.py
@@ -59,15 +59,13 @@
     acts_hbm,
     cot_in,
     mom_hbm,
-    new_hbm,
-    upd_hbm,
+    new_mix,
+    upd_mix,
     acts_in,
     mom_raw,
     mom_in,
     new_out,
     upd_out,
-    new_mix,
-    upd_mix,
     tok_in,
     tok_r,
     t2_s,
@@ -492,8 +490,6 @@
 
     for expert in range(EXPERTS_HERE):
         interleave(new_out, new_mix, expert)
-    new_store = pltpu.make_async_copy(new_mix, new_hbm, local_sem.at[8])
-    new_store.start()
 
     tok_copy(0, 1).wait_send()
 
@@ -515,33 +511,37 @@
         return carry
 
     lax.fori_loop(1, CHIPS, finish, 0)
-    upd_local.wait()
-
-    def wait_upd(i, carry):
-        source = lax.rem(chip + i, CHIPS)
-        remote(
-            upd_s.at[0],
-            upd_out.at[matrix(source)],
-            upd_ss.at[i],
-            upd_rs.at[matrix(source)],
-            source * 2 + core,
-            exp,
-        ).wait_recv()
-        return carry
-
-    lax.fori_loop(1, CHIPS, wait_upd, 0)
-    for expert in range(EXPERTS_HERE):
-        interleave(upd_out, upd_mix, expert)
-    upd_store = pltpu.make_async_copy(upd_mix, upd_hbm, local_sem.at[9])
-    upd_store.start()
+    def collect(i, carry):
+        side = lax.rem(x + i // 2, 2)
+        half = lax.rem(y // 2 + i, 2)
+        for kind in range(2):
+            source = 2 * (2 * half + kind) + side
+
+            @pl.when(source == chip)
+            def _():
+                upd_local.wait()
+
+            @pl.when(source != chip)
+            def _():
+                remote(
+                    upd_s.at[0],
+                    upd_out.at[matrix(source)],
+                    upd_ss.at[0],
+                    upd_rs.at[matrix(source)],
+                    source * 2 + core,
+                    exp,
+                ).wait_recv()
+
+        interleave(upd_out, upd_mix, 2 * side + half)
+        return carry
+
+    lax.fori_loop(0, EXPERTS_HERE, collect, 0)
 
     def finish_upd(i, carry):
         upd_copy(i).wait_send()
         return carry
 
     lax.fori_loop(1, CHIPS, finish_upd, 0)
-    new_store.wait()
-    upd_store.wait()
 
 
 def on_device(acts, cotangent, counts, momentum):
@@ -555,22 +555,20 @@
     mixed = (SHARD, EXPERTS_HERE, 2, HIDDEN)
     return pl.pallas_call(
         kernel,
-        out_shape=(jax.ShapeDtypeStruct(mixed, bf16),) * 2,
+        out_shape=(pltpu.VMEM(mixed, bf16),) * 2,
         in_specs=[
             pl.BlockSpec(memory_space=pltpu.SMEM),
             pl.BlockSpec(memory_space=pl.ANY),
             pl.BlockSpec(memory_space=pl.ANY),
             pl.BlockSpec(memory_space=pl.ANY),
         ],
-        out_specs=(pl.BlockSpec(memory_space=pl.ANY),) * 2,
+        out_specs=(pl.BlockSpec(memory_space=pltpu.VMEM),) * 2,
         scratch_shapes=[
             vmem((EXP * EXPERTS_HERE, SLOTS, WIDTH), bf16),
             vmem(mixed, bf16),
             vmem(rows, bf16),
             vmem(rows, bf16),
             vmem(rows, bf16),
-            vmem(mixed, bf16),
-            vmem(mixed, bf16),
             vmem((EXP, SIDES, SIDE_ROWS, WIDTH), bf16),
             vmem((SIDES, EXP, SIDE_ROWS, WIDTH), bf16),
             vmem((SIDE_EXPERTS, 2, SIDES * TOKENS, HALF), bf16),
@@ -606,7 +604,7 @@
             dma((CHIPS,)),
             dma((2,)),
             dma((2,)),
-            dma((10,)),
+            dma((8,)),
         ],
         compiler_params=pltpu.CompilerParams(
             collective_id=0, has_side_effects=True, vmem_limit_bytes=60 << 20

time: 92.8 us -> 89.3 us (0.962)
  local copies, waits for them, and re-layouts: 4.89 us -> 2.29 us
    unnamed x4 -> x2, local copies, waits for them, and re-layouts: 4.89 us -> 2.29 us
where the time goes in v4:
time: 89.3 us; the launch traced here: 89.2 us
  Pallas kernels  86.2 us (97%)
  local copies, waits for them, and re-layouts  2.29 us (3%)
    pallas_call x1, Pallas kernels, on_device(): pl.pallas_call(kernel, out_shape=(pltpu.VMEM(mixed, bf16),) * 2, in_specs...  86.2 us
    unnamed x2, local copies, waits for them, and re-layouts  2.29 us

profile of v4, /device:TPU:1, one launch (start us, length us, event | category | flops | bytes accessed | tf_op | source)
XLA Modules:
  0.0 89.2 jit_solution(8848669613882636281)
XLA Ops:
  0.6 86.2 %muon_owner.1 = (bf16[128,4,2,768]{3,2,1,0:T(2,128)(2,1)S(1)}, bf16[128,4,2,768]{3,2,1,0:T(2,128)(2,1)S(1)}) custom-call(s32[64]{0:T(128)} %bitcast.5, bf16[64,2,2048]{2,1,0:T(2,128)(2,1)} %bitcast.3, bf16[8,32,768]{2,1,0:T(8,128)(2,1)} %bitcast.4, bf16[128,4,2,768]{3,2,1,0:T(2,128)(2,1)} %mom_hbm.1), custom_call_target="tpu_custom_call" | custom-call | tf_op jit(solution)/shard_map/muon_owner/pallas_call | solution.py:556
  86.9 1.1 %copy.8 = bf16[128,4,2,768]{3,2,1,0:T(2,128)(2,1)} copy(bf16[128,4,2,768]{3,2,1,0:T(2,128)(2,1)S(1)} %get-tuple-element.2) | data formatting | bytes 3145728
  88.0 1.1 %copy.9 = bf16[128,4,2,768]{3,2,1,0:T(2,128)(2,1)} copy(bf16[128,4,2,768]{3,2,1,0:T(2,128)(2,1)S(1)} %get-tuple-element.3) | data formatting | bytes 3145728

commit v5 on v4

--- a/solution.py
+++ b/solution.py
@@ -29,6 +29,9 @@
 HIDDEN = 768
 TOKENS = 32
 TILE = 256
+EARLY = 4
+LEADER = 0
+MESSENGER = 1
 
 MESH = pl.DeviceIdType.MESH
 f32 = jnp.float32
@@ -102,6 +105,8 @@
     pair_ss,
     pair_rs,
     local_sem,
+    group_sem,
+    all_sem,
 ):
     rep = lax.axis_index("rep")
     exp = lax.axis_index("exp")
@@ -122,17 +127,40 @@
             pltpu.get_barrier_semaphore(), inc=1, device_id=(to_rep, to_exp), device_id_type=MESH
         )
 
+    @pl.when(rep != LEADER)
+    def _():
+        signal(LEADER, exp)
+
+    near = jnp.where(rep == LEADER, MESSENGER, rep)
+    cross = jnp.where(rep_x == LEADER, MESSENGER, rep_x)
+
     def greet(i, carry):
-        signal(rep, lax.rem(exp + i, EXP))
-        signal(lax.rem(rep + i, REP), exp)
-        signal(rep_x, lax.rem(exp + i, EXP))
-        return carry
-
-    lax.fori_loop(1, 16, greet, 0)
+        to = lax.rem(exp + i, EXP)
+        signal(near, to)
+        signal(cross, to)
+        return carry
+
+    @pl.when(rep_x != LEADER)
+    def _():
+        signal(rep_x, exp)
+
+    lax.fori_loop(1, EXP, greet, 0)
     acts_load = pltpu.make_async_copy(acts_hbm, acts_in, local_sem.at[6])
     mom_load = pltpu.make_async_copy(mom_hbm, mom_raw, local_sem.at[7])
     acts_load.start()
     mom_load.start()
+
+    @pl.when(rep == LEADER)
+    def _():
+        pl.semaphore_wait(pltpu.get_barrier_semaphore(), REP - 1)
+
+        def tell(i, carry):
+            pl.semaphore_signal(
+                group_sem, inc=1, device_id=(lax.rem(rep + i, REP), exp), device_id_type=MESH
+            )
+            return carry
+
+        lax.fori_loop(1, REP, tell, 0)
 
     row = lax.broadcasted_iota(jnp.int32, (SIDE_ROWS, WIDTH), 0)
 
@@ -147,7 +175,9 @@
 
     acts_load.wait()
     lax.fori_loop(0, EXP * SIDES, mask, 0)
-    pl.semaphore_wait(pltpu.get_barrier_semaphore(), 45)
+    mom_load.wait()
+    for expert in range(EXPERTS_HERE):
+        mom_in[2 * expert : 2 * expert + 2] = jnp.swapaxes(mom_raw[:, expert], 0, 1)
 
     def tok_copy(i, other):
         to = lax.rem(exp + i, EXP)
@@ -172,7 +202,8 @@
         )
 
     def mom_copy(i):
-        to = lax.rem(chip + i, CHIPS)
+        step, turned = (i, 1 - x) if i < YS else (i - YS + 1, x)
+        to = 2 * lax.rem(y + step, YS) + turned
         return remote(
             mom_in.at[matrix(to)],
             mom_r.at[chip],
@@ -186,6 +217,42 @@
     cot_local = pltpu.make_async_copy(cot_in.at[mine], cot_r.at[peer, x], local_sem.at[1])
     mom_local = pltpu.make_async_copy(mom_in.at[mine], mom_r.at[chip], local_sem.at[2])
 
+    def start_cot(i, carry):
+        cot_copy(i).start()
+        return carry
+
+    def hear_group(listens):
+        @pl.when(listens)
+        def _():
+            pl.semaphore_wait(group_sem, 1)
+
+        lax.fori_loop(1, CHIPS, start_cot, 0)
+
+    early = exp // 2 < EARLY
+
+    @pl.when(early)
+    def _():
+        hear_group(rep != LEADER)
+        for i in range(4, 7):
+            mom_copy(i).start()
+
+    @pl.when(rep == LEADER)
+    def _():
+        pl.semaphore_wait(all_sem, 1)
+
+    @pl.when(jnp.logical_and(rep == MESSENGER, jnp.logical_not(early)))
+    def _():
+        pl.semaphore_wait(group_sem, 1)
+
+    @pl.when(rep == MESSENGER)
+    def _():
+        pl.semaphore_wait(pltpu.get_barrier_semaphore(), 4 * (EXP - 1) + 1)
+        pl.semaphore_signal(all_sem, inc=1, device_id=(LEADER, exp), device_id_type=MESH)
+
+    @pl.when(jnp.logical_and(rep != LEADER, rep != MESSENGER))
+    def _():
+        pl.semaphore_wait(pltpu.get_barrier_semaphore(), 2 * (EXP - 1) + 1)
+
     tok_copy(0, 1).start()
 
     def start_tok(i, carry):
@@ -195,21 +262,15 @@
 
     lax.fori_loop(1, EXP, start_tok, 0)
 
-    def start_cot(i, carry):
-        cot_copy(i).start()
-        return carry
-
-    lax.fori_loop(1, CHIPS, start_cot, 0)
-
-    mom_load.wait()
-    for expert in range(EXPERTS_HERE):
-        mom_in[2 * expert : 2 * expert + 2] = jnp.swapaxes(mom_raw[:, expert], 0, 1)
-
-    def start_mom(i, carry):
+    @pl.when(jnp.logical_not(early))
+    def _():
+        hear_group(jnp.logical_and(rep != LEADER, rep != MESSENGER))
+        for i in range(4, 7):
+            mom_copy(i).start()
+
+    for i in range(4):
         mom_copy(i).start()
-        return carry
-
-    lax.fori_loop(1, CHIPS, start_mom, 0)
+
     tok_local.start()
     cot_local.start()
     mom_local.start()
@@ -501,11 +562,12 @@
     lax.fori_loop(1, EXP, finish_tok, 0)
 
     forward(chip).wait_send()
+    for i in range(7):
+        mom_copy(i).wait_send()
 
     def finish(i, carry):
         cot_copy(i).wait_send()
         forward(lax.rem(chip + i, CHIPS)).wait_send()
-        mom_copy(i).wait_send()
         t2_copy(i).wait_send()
         new_copy(i).wait_send()
         return carry
@@ -605,6 +667,8 @@
             dma((2,)),
             dma((2,)),
             dma((8,)),
+            pltpu.SemaphoreType.REGULAR,
+            pltpu.SemaphoreType.REGULAR,
         ],
         compiler_params=pltpu.CompilerParams(
             collective_id=0, has_side_effects=True, vmem_limit_bytes=60 << 20

time: 89.3 us -> 88.7 us (level)
  no operation moved by 1% of the time
where the time goes in v5:
time: 88.7 us; the launch traced here: 88.6 us
  Pallas kernels  85.7 us (97%)
  local copies, waits for them, and re-layouts  2.29 us (3%)
    pallas_call x1, Pallas kernels, on_device(): pl.pallas_call(kernel, out_shape=(pltpu.VMEM(mixed, bf16),) * 2, in_specs...  85.7 us
    unnamed x2, local copies, waits for them, and re-layouts  2.29 us

profile of v5, /device:TPU:1, one launch (start us, length us, event | category | flops | bytes accessed | tf_op | source)
XLA Modules:
  0.0 88.6 jit_solution(9912816246476997205)
XLA Ops:
  0.6 85.7 %muon_owner.1 = (bf16[128,4,2,768]{3,2,1,0:T(2,128)(2,1)S(1)}, bf16[128,4,2,768]{3,2,1,0:T(2,128)(2,1)S(1)}) custom-call(s32[64]{0:T(128)} %bitcast.5, bf16[64,2,2048]{2,1,0:T(2,128)(2,1)} %bitcast.3, bf16[8,32,768]{2,1,0:T(8,128)(2,1)} %bitcast.4, bf16[128,4,2,768]{3,2,1,0:T(2,128)(2,1)} %mom_hbm.1), custom_call_target="tpu_custom_call" | custom-call | tf_op jit(solution)/shard_map/muon_owner/pallas_call | solution.py:618
  86.3 1.1 %copy.8 = bf16[128,4,2,768]{3,2,1,0:T(2,128)(2,1)} copy(bf16[128,4,2,768]{3,2,1,0:T(2,128)(2,1)S(1)} %get-tuple-element.2) | data formatting | bytes 3145728
  87.4 1.1 %copy.9 = bf16[128,4,2,768]{3,2,1,0:T(2,128)(2,1)} copy(bf16[128,4,2,768]{3,2,1,0:T(2,128)(2,1)S(1)} %get-tuple-element.3) | data formatting | bytes 3145728

commit v6 on v5

--- a/solution.py
+++ b/solution.py
@@ -127,6 +127,11 @@
             pltpu.get_barrier_semaphore(), inc=1, device_id=(to_rep, to_exp), device_id_type=MESH
         )
 
+    acts_load = pltpu.make_async_copy(acts_hbm, acts_in, local_sem.at[6])
+    mom_load = pltpu.make_async_copy(mom_hbm, mom_raw, local_sem.at[7])
+    acts_load.start()
+    mom_load.start()
+
     @pl.when(rep != LEADER)
     def _():
         signal(LEADER, exp)
@@ -145,10 +150,6 @@
         signal(rep_x, exp)
 
     lax.fori_loop(1, EXP, greet, 0)
-    acts_load = pltpu.make_async_copy(acts_hbm, acts_in, local_sem.at[6])
-    mom_load = pltpu.make_async_copy(mom_hbm, mom_raw, local_sem.at[7])
-    acts_load.start()
-    mom_load.start()
 
     @pl.when(rep == LEADER)
     def _():
@@ -175,10 +176,6 @@
 
     acts_load.wait()
     lax.fori_loop(0, EXP * SIDES, mask, 0)
-    mom_load.wait()
-    for expert in range(EXPERTS_HERE):
-        mom_in[2 * expert : 2 * expert + 2] = jnp.swapaxes(mom_raw[:, expert], 0, 1)
-
     def tok_copy(i, other):
         to = lax.rem(exp + i, EXP)
         return remote(
@@ -228,10 +225,16 @@
 
         lax.fori_loop(1, CHIPS, start_cot, 0)
 
+    def split_momentum():
+        mom_load.wait()
+        for expert in range(EXPERTS_HERE):
+            mom_in[2 * expert : 2 * expert + 2] = jnp.swapaxes(mom_raw[:, expert], 0, 1)
+
     early = exp // 2 < EARLY
 
     @pl.when(early)
     def _():
+        split_momentum()
         hear_group(rep != LEADER)
         for i in range(4, 7):
             mom_copy(i).start()
@@ -265,6 +268,7 @@
     @pl.when(jnp.logical_not(early))
     def _():
         hear_group(jnp.logical_and(rep != LEADER, rep != MESSENGER))
+        split_momentum()
         for i in range(4, 7):
             mom_copy(i).start()
 

time: 88.7 us -> 88.7 us (level)
  no operation moved by 1% of the time
where the time goes in v6:
time: 88.7 us; the launch traced here: 88.6 us
  Pallas kernels  85.6 us (97%)
  local copies, waits for them, and re-layouts  2.29 us (3%)
    pallas_call x1, Pallas kernels, on_device(): pl.pallas_call(kernel, out_shape=(pltpu.VMEM(mixed, bf16),) * 2, in_specs...  85.6 us
    unnamed x2, local copies, waits for them, and re-layouts  2.29 us

profile of v6, /device:TPU:1, one launch (start us, length us, event | category | flops | bytes accessed | tf_op | source)
XLA Modules:
  0.0 88.6 jit_solution(16850535819710934072)
XLA Ops:
  0.6 85.6 %muon_owner.1 = (bf16[128,4,2,768]{3,2,1,0:T(2,128)(2,1)S(1)}, bf16[128,4,2,768]{3,2,1,0:T(2,128)(2,1)S(1)}) custom-call(s32[64]{0:T(128)} %bitcast.5, bf16[64,2,2048]{2,1,0:T(2,128)(2,1)} %bitcast.3, bf16[8,32,768]{2,1,0:T(8,128)(2,1)} %bitcast.4, bf16[128,4,2,768]{3,2,1,0:T(2,128)(2,1)} %mom_hbm.1), custom_call_target="tpu_custom_call" | custom-call | tf_op jit(solution)/shard_map/muon_owner/pallas_call | solution.py:622
  86.3 1.1 %copy.8 = bf16[128,4,2,768]{3,2,1,0:T(2,128)(2,1)} copy(bf16[128,4,2,768]{3,2,1,0:T(2,128)(2,1)S(1)} %get-tuple-element.2) | data formatting | bytes 3145728
  87.4 1.1 %copy.9 = bf16[128,4,2,768]{3,2,1,0:T(2,128)(2,1)} copy(bf16[128,4,2,768]{3,2,1,0:T(2,128)(2,1)S(1)} %get-tuple-element.3) | data formatting | bytes 3145728

commit v7 on v6

--- a/solution.py
+++ b/solution.py
@@ -419,30 +419,33 @@
     sq_s[...] = jnp.zeros_like(sq_s)
     cots = cot_r[...].reshape(REP * TOKENS, HIDDEN)
 
-    def gradient(i):
+    def gradient(i, sent):
         at = lax.rem(chip + i, CHIPS)
         columns = pl.ds(pl.multiple_of(at * SHARD, SHARD), SHARD)
         feats = t2_r[:, :, columns].reshape(REP * TOKENS, SHARD)
         grad = dot_rows(feats, cots)
         mom = decay_rate * mom_r[at].astype(f32) + grad
         new_s[at] = mom.astype(bf16)
+        sent(at)
         nest = (grad + decay_rate * mom).astype(bf16)
         nest_s[at] = nest
-        wide = nest.astype(f32)
+
+    def add_squares(at, carry):
+        wide = nest_s[at].astype(f32)
         squares = jnp.sum((wide * wide).reshape(SHARD // 8, 8, HIDDEN // 128, 128), axis=(0, 2))
         sq_s[...] += squares
+        return carry
 
     def gradient_send(i, carry):
         wait_mom(lax.rem(chip + i, CHIPS))
-        gradient(i)
-        new_copy(i).start()
+        gradient(i, lambda at: new_copy(i).start())
         return carry
 
     lax.fori_loop(1, CHIPS, gradient_send, 0)
     mom_local.wait()
-    gradient(0)
     new_local = pltpu.make_async_copy(new_s.at[chip], new_out.at[mine], local_sem.at[4])
-    new_local.start()
+    gradient(0, lambda at: new_local.start())
+    lax.fori_loop(0, CHIPS, add_squares, 0)
 
     def gram_tile(j, carry):
         columns = pl.ds(pl.multiple_of(j * TILE, TILE), TILE)

time: 88.7 us -> 89.3 us (level)
  no operation moved by 1% of the time
where the time goes in v7:
time: 89.3 us; the launch traced here: 89.2 us
  Pallas kernels  86.3 us (97%)
  local copies, waits for them, and re-layouts  2.29 us (3%)
    pallas_call x1, Pallas kernels, on_device(): pl.pallas_call(kernel, out_shape=(pltpu.VMEM(mixed, bf16),) * 2, in_specs...  86.3 us
    unnamed x2, local copies, waits for them, and re-layouts  2.29 us

profile of v7, /device:TPU:1, one launch (start us, length us, event | category | flops | bytes accessed | tf_op | source)
XLA Modules:
  0.0 89.2 jit_solution(5070153671255223464)
XLA Ops:
  0.6 86.3 %muon_owner.1 = (bf16[128,4,2,768]{3,2,1,0:T(2,128)(2,1)S(1)}, bf16[128,4,2,768]{3,2,1,0:T(2,128)(2,1)S(1)}) custom-call(s32[64]{0:T(128)} %bitcast.5, bf16[64,2,2048]{2,1,0:T(2,128)(2,1)} %bitcast.3, bf16[8,32,768]{2,1,0:T(8,128)(2,1)} %bitcast.4, bf16[128,4,2,768]{3,2,1,0:T(2,128)(2,1)} %mom_hbm.1), custom_call_target="tpu_custom_call" | custom-call | tf_op jit(solution)/shard_map/muon_owner/pallas_call | solution.py:625
  86.9 1.1 %copy.8 = bf16[128,4,2,768]{3,2,1,0:T(2,128)(2,1)} copy(bf16[128,4,2,768]{3,2,1,0:T(2,128)(2,1)S(1)} %get-tuple-element.2) | data formatting | bytes 3145728
  88.1 1.1 %copy.9 = bf16[128,4,2,768]{3,2,1,0:T(2,128)(2,1)} copy(bf16[128,4,2,768]{3,2,1,0:T(2,128)(2,1)S(1)} %get-tuple-element.3) | data formatting | bytes 3145728

commit v8 on v6

--- a/solution.py
+++ b/solution.py
@@ -410,8 +410,12 @@
     lax.fori_loop(1, CHIPS, wait_t2, 0)
     t2_local.wait()
 
+    def turn_of(i):
+        step = jnp.where(i < YS, i, i - YS)
+        return 2 * lax.rem(y + step, YS) + jnp.where(i < YS, x, 1 - x)
+
     def new_copy(i):
-        to = lax.rem(chip + i, CHIPS)
+        to = turn_of(i)
         return remote(
             new_s.at[to], new_out.at[mine], new_ss.at[i], new_rs.at[mine], to * 2 + core, exp
         )
@@ -420,7 +424,7 @@
     cots = cot_r[...].reshape(REP * TOKENS, HIDDEN)
 
     def gradient(i):
-        at = lax.rem(chip + i, CHIPS)
+        at = turn_of(i)
         columns = pl.ds(pl.multiple_of(at * SHARD, SHARD), SHARD)
         feats = t2_r[:, :, columns].reshape(REP * TOKENS, SHARD)
         grad = dot_rows(feats, cots)
@@ -433,7 +437,7 @@
         sq_s[...] += squares
 
     def gradient_send(i, carry):
-        wait_mom(lax.rem(chip + i, CHIPS))
+        wait_mom(turn_of(i))
         gradient(i)
         new_copy(i).start()
         return carry

time: 88.7 us -> 89.3 us (level)
  no operation moved by 1% of the time
where the time goes in v8:
time: 89.3 us; the launch traced here: 89.1 us
  Pallas kernels  86.2 us (97%)
  local copies, waits for them, and re-layouts  2.29 us (3%)
    pallas_call x1, Pallas kernels, on_device(): pl.pallas_call(kernel, out_shape=(pltpu.VMEM(mixed, bf16),) * 2, in_specs...  86.2 us
    unnamed x2, local copies, waits for them, and re-layouts  2.29 us

profile of v8, /device:TPU:1, one launch (start us, length us, event | category | flops | bytes accessed | tf_op | source)
XLA Modules:
  0.0 89.1 jit_solution(10028673011318452287)
XLA Ops:
  0.6 86.2 %muon_owner.1 = (bf16[128,4,2,768]{3,2,1,0:T(2,128)(2,1)S(1)}, bf16[128,4,2,768]{3,2,1,0:T(2,128)(2,1)S(1)}) custom-call(s32[64]{0:T(128)} %bitcast.5, bf16[64,2,2048]{2,1,0:T(2,128)(2,1)} %bitcast.3, bf16[8,32,768]{2,1,0:T(8,128)(2,1)} %bitcast.4, bf16[128,4,2,768]{3,2,1,0:T(2,128)(2,1)} %mom_hbm.1), custom_call_target="tpu_custom_call" | custom-call | tf_op jit(solution)/shard_map/muon_owner/pallas_call | solution.py:626
  86.8 1.1 %copy.8 = bf16[128,4,2,768]{3,2,1,0:T(2,128)(2,1)} copy(bf16[128,4,2,768]{3,2,1,0:T(2,128)(2,1)S(1)} %get-tuple-element.2) | data formatting | bytes 3145728
  88.0 1.1 %copy.9 = bf16[128,4,2,768]{3,2,1,0:T(2,128)(2,1)} copy(bf16[128,4,2,768]{3,2,1,0:T(2,128)(2,1)S(1)} %get-tuple-element.3) | data formatting | bytes 3145728
